TPU v7x, 128 devices: a whole 4x4x4 slice. The times are simulated.
128 devices in a mesh: slab: 32 (over x, z, core), store: 4 (over y).
Axes of the slice: x: 4, y: 4, z: 4, core: 2. Of those that a mesh axis runs over, the one named last changes fastest.
Arguments:
- basis: bfloat16 [786432, 1024], P('slab', 'store'), may hold values from -6 to 6
- panels: bfloat16 [1024, 512], P(('slab', 'store')), may hold values from -0.1875 to 0.1875
- block_dest: int32 [2048], P(('slab', 'store')), may hold values from 0 to 2047, as said below
Outputs:
- ritz: bfloat16 [786432, 512], P(('slab', 'store'))
Inputs may be any that keep to these rules, and one draw needn't show every extreme that they name: block_dest is a permutation of the row blocks. It keeps a block's index along store: block b lies in the sub-slab (b // 16) % 4 and so does block_dest[b]. The 16 blocks of one sub-slab go to 16 reader slabs, exactly 1 to each, and every reader sub-slab receives its blocks from 16 sub-slabs.
All inputs are finite; a program needn't handle non-finite values.
Results may differ from a plain program's by a relative error of at most 0.001.
Values may be sent and summed in bfloat16 or wider, within the bound.
A program may use at most 192 MiB of HBM per device.

v0:
```python
import jax
import jax.numpy as jnp
from jax import lax
from jax.sharding import PartitionSpec as P


def rebalance(blocks, block_dest):
    nblocks = blocks.shape[0]
    n_slab = lax.axis_size("slab")
    n_store = lax.axis_size("store")
    per_peer = 2 * nblocks // n_slab
    slots = n_slab * per_peer
    target = block_dest // (nblocks * n_store)
    onehot = (target[:, None] == jnp.arange(n_slab, dtype=jnp.int32)[None, :]).astype(jnp.int32)
    before = jnp.cumsum(onehot, axis=0) - onehot
    order_in = jnp.sum(onehot * before, axis=1)
    slot_of = target * per_peer + order_in
    chosen = jnp.arange(slots, dtype=jnp.int32)[:, None] == slot_of[None, :]
    outgoing = jnp.dot(
        chosen.astype(jnp.bfloat16), blocks, preferred_element_type=jnp.float32
    ).astype(jnp.bfloat16)
    labels = jnp.sum(jnp.where(chosen, block_dest[None, :] + 1, 0), axis=1) - 1
    arrived, arrived_labels = (
        lax.all_to_all(outgoing, "slab", split_axis=0, concat_axis=0, tiled=True),
        lax.all_to_all(labels, "slab", split_axis=0, concat_axis=0, tiled=True),
    )
    device = lax.axis_index("slab") * n_store + lax.axis_index("store")
    wanted = device * nblocks + jnp.arange(nblocks, dtype=jnp.int32)
    picker = (arrived_labels[None, :] == wanted[:, None]).astype(jnp.bfloat16)
    return jnp.dot(picker, arrived, preferred_element_type=jnp.float32).astype(jnp.bfloat16)


def body(basis, panels, block_dest):
    coeffs = lax.all_gather(panels, ("slab", "store"), axis=0, tiled=True)
    sub_rows = lax.all_to_all(basis, "store", split_axis=0, concat_axis=1, tiled=True)
    nblocks = block_dest.shape[0]
    brows = sub_rows.shape[0] // nblocks
    ncols = coeffs.shape[1]
    product = jnp.dot(sub_rows, coeffs, preferred_element_type=jnp.float32).astype(jnp.bfloat16)
    ritz = rebalance(product.reshape(nblocks, brows * ncols), block_dest).reshape(
        nblocks * brows, ncols
    )
    return ritz


def solution(mesh):
    in_specs = (P("slab", "store"), P(("slab", "store"), None), P(("slab", "store")))
    out_specs = P(("slab", "store"), None)
    return jax.shard_map(body, mesh=mesh, in_specs=in_specs, out_specs=out_specs, check_vma=False)
```

profile of v0, /device:TPU:36, one launch (start us, length us, event | category | flops | bytes accessed | tf_op | source)
XLA Modules:
  0.0 506.8 jit_solution(6162764039467779287)
XLA Ops:
  6.5 6.5 %all-to-all-start.1 = ((bf16[4,6144,256]{2,1,0:T(8,128)(2,1)}), bf16[4,6144,256]{2,1,0:T(8,128)(2,1)}, u32[]{:S(2)}, u32[]{:S(2)}) async-start(bf16[4,6144,256]{2,1,0:T(8,128)(2,1)} %bitcast.13), calls=%async_computation.1 | async-start | bytes 25165824 | tf_op jit(solution)/shard_map/all_to_all | solution.py:35
  13.0 0.0 all-gather.2.cloned.1.call-start
  13.1 0.7 all-gather.2.cloned.1.call-update
  13.7 0.0 copy-done
  13.8 0.1 fusion.3
  13.9 0.2 select_reduce_fusion.1
  14.1 0.1 select_reduce_fusion
  14.2 0.7 copy.11
  14.9 138.7 %all-to-all-done.1 = bf16[4,6144,256]{2,1,0:T(8,128)(2,1)} async-done(((bf16[4,6144,256]{2,1,0:T(8,128)(2,1)}), bf16[4,6144,256]{2,1,0:T(8,128)(2,1)}, u32[]{:S(2)}, u32[]{:S(2)}) %all-to-all-start.1) | async-done | bytes 12582944 | tf_op jit(solution)/shard_map/all_to_all | solution.py:35
  153.6 8.0 %all-to-all-start = ((s32[32,1,1]{2,1,0:T(1,128)}), s32[32,1,1]{2,1,0:T(1,128)S(1)}, u32[]{:S(2)}, u32[]{:S(2)}) async-start(s32[32,1,1]{2,1,0:T(1,128)} %copy.11), calls=%async_computation | async-start | bytes 32768 | tf_op jit(solution)/shard_map/all_to_all | solution.py:25
  161.6 16.7 %copy.12 = bf16[6144,4,256]{0,2,1:T(8,128)(2,1)} copy(bf16[6144,4,256]{2,0,1:T(8,128)(2,1)} %bitcast.2) | data formatting | bytes 25165824 | tf_op jit(solution)/shard_map/all_to_all | solution.py:35
  178.3 11.7 %convolution_convert_fusion.2 = bf16[6144,512]{1,0:T(8,128)(2,1)} fusion(bf16[6144,1024]{0,1:T(8,128)(2,1)} %bitcast.14, bf16[1024,512]{1,0:T(8,128)(2,1)} %all-gather.2.cloned.1.call-done), kind=kOutput, calls=%fused_computation.5 | convolution fusion | flops 6445596672 | bytes 19922944 | tf_op jit(solution)/shard_map/dot_general | solution.py:39
  190.0 6.4 %reshape.32 = bf16[16,196608]{1,0:T(8,128)(2,1)} reshape(bf16[6144,512]{1,0:T(8,128)(2,1)} %convolution_convert_fusion.2) | data formatting | bytes 12582912 | tf_op jit(solution)/shard_map/reshape | solution.py:40
  196.4 8.4 %fusion = bf16[32,1,196608]{2,0,1:T(8,128)(2,1)} fusion(bf16[16,196608]{1,0:T(8,128)(2,1)} %reshape.32, s32[16]{0:T(128)S(1)} %add.30), kind=kOutput, calls=%fused_computation.1 | convolution fusion | flops 207618560 | bytes 18874432 | tf_op jit(solution)/shard_map/dot_general | solution.py:19
  204.8 0.5 broadcast.46
  205.3 15.1 %reduce.1 = bf16[32,196608]{1,0:T(8,128)(2,1)} reduce(bf16[32,1,196608]{2,0,1:T(8,128)(2,1)} %fusion, bf16[]{:T(256)} %broadcast.46), dimensions={1}, to_apply=%copy.13.reduce_sub_computation | reduce | bytes 25165826 | tf_op jit(solution)/shard_map/all_to_all | solution.py:24
  220.5 15.2 %reshape.35 = bf16[32,2,98304]{2,1,0:T(2,128)(2,1)} reshape(bf16[32,196608]{1,0:T(8,128)(2,1)} %reduce.1) | data formatting | bytes 25165824
  235.7 0.0 all-to-all-done
  235.7 7.4 %all-to-all-start.2 = ((bf16[32,2,98304]{2,1,0:T(2,128)(2,1)}), bf16[32,2,98304]{2,1,0:T(2,128)(2,1)}, u32[]{:S(2)}, u32[]{:S(2)}) async-start(bf16[32,2,98304]{2,1,0:T(2,128)(2,1)} %reshape.35), calls=%async_computation.2 | async-start | bytes 25165824 | tf_op jit(solution)/shard_map/all_to_all | solution.py:24
  243.1 0.7 reduce
  243.8 197.7 %all-to-all-done.2 = bf16[32,2,98304]{2,1,0:T(2,128)(2,1)} async-done(((bf16[32,2,98304]{2,1,0:T(2,128)(2,1)}), bf16[32,2,98304]{2,1,0:T(2,128)(2,1)}, u32[]{:S(2)}, u32[]{:S(2)}) %all-to-all-start.2) | async-done | bytes 12582944 | tf_op jit(solution)/shard_map/all_to_all | solution.py:24
  441.5 27.5 %reshape.36 = bf16[32,1,196608]{2,1,0:T(2,128)(2,1)} reshape(bf16[32,2,98304]{2,1,0:T(2,128)(2,1)} %all-to-all-done.2) | data formatting | bytes 25165824
  469.0 24.5 %convolution_convert_fusion.1 = bf16[16,196608]{1,0:T(8,128)(2,1)} fusion(bf16[32,1,196608]{2,1,0:T(2,128)(2,1)} %reshape.36, s32[32]{0:T(128)S(1)} %reduce, s32[16]{0:T(128)S(1)} %iota_add_fusion), kind=kOutput, calls=%fused_computation.2 | convolution fusion | flops 204472832 | bytes 18874560 | tf_op jit(solution)/shard_map/dot_general | solution.py:30
  493.5 6.4 %reshape.33 = bf16[6144,512]{1,0:T(8,128)(2,1)} reshape(bf16[16,196608]{1,0:T(8,128)(2,1)} %convolution_convert_fusion.1) | data formatting | bytes 12582912 | tf_op jit(solution)/shard_map/reshape | solution.py:40
  (7 shorter events, 0.1 us)
Async XLA Ops:
  6.5 7.2 %copy-start = (s32[16]{0:T(128)S(1)}, s32[16]{0:T(128)}, u32[]{:S(2)}) copy-start(s32[16]{0:T(128)} %param.5) | copy-start | bytes 196
  6.5 147.0 %all-to-all-start.1 = ((bf16[4,6144,256]{2,1,0:T(8,128)(2,1)}), bf16[4,6144,256]{2,1,0:T(8,128)(2,1)}, u32[]{:S(2)}, u32[]{:S(2)}) async-start(bf16[4,6144,256]{2,1,0:T(8,128)(2,1)} %bitcast.13), calls=%async_computation.1 | async-start | bytes 25165824 | tf_op jit(solution)/shard_map/all_to_all | solution.py:35
  13.0 165.3 %all-gather.2.cloned.1.call-start = ((), (), s32[]{:S(2)}) async-start(), calls=%async_computation.3 | async-start | bytes 1056768 | tf_op jit(solution)/shard_map/all_gather | solution.py:34
  153.6 82.1 %all-to-all-start = ((s32[32,1,1]{2,1,0:T(1,128)}), s32[32,1,1]{2,1,0:T(1,128)S(1)}, u32[]{:S(2)}, u32[]{:S(2)}) async-start(s32[32,1,1]{2,1,0:T(1,128)} %copy.11), calls=%async_computation | async-start | bytes 32768 | tf_op jit(solution)/shard_map/all_to_all | solution.py:25
  235.7 205.8 %all-to-all-start.2 = ((bf16[32,2,98304]{2,1,0:T(2,128)(2,1)}), bf16[32,2,98304]{2,1,0:T(2,128)(2,1)}, u32[]{:S(2)}, u32[]{:S(2)}) async-start(bf16[32,2,98304]{2,1,0:T(2,128)(2,1)} %reshape.35), calls=%async_computation.2 | async-start | bytes 25165824 | tf_op jit(solution)/shard_map/all_to_all | solution.py:24
Sparse Core Ops, SparseCore 0:
  16.6 65.0 all-gather.1
where the time goes:
time: 508 us; the launch traced here: 507 us
  waiting for transfers between devices  337 us (66%)
  local copies, waits for them, and re-layouts  73.4 us (14%)
  matrix products  44.7 us (9%)
  starting transfers between devices  21.9 us (4%)
  other arithmetic  16.2 us (3%)
  between operations  13.5 us (3%)
    all_to_all x1, waiting for transfers between devices, rebalance(): lax.all_to_all(outgoing, 'slab', split_axis=0, concat_axis=0, tiled=True)  198 us
    all_to_all x1, waiting for transfers between devices, body(): lax.all_to_all(basis, 'store', split_axis=0, concat_axis=1, tiled=True)  139 us
    unnamed x4, local copies, waits for them, and re-layouts  42.7 us
    dot_general x1, matrix products, rebalance(): jnp.dot(picker, arrived, preferred_element_type=jnp.float32)  24.5 us
    all_to_all x1, local copies, waits for them, and re-layouts, body(): lax.all_to_all(basis, 'store', split_axis=0, concat_axis=1, tiled=True)  16.7 us
    all_to_all x1, other arithmetic, rebalance(): lax.all_to_all(outgoing, 'slab', split_axis=0, concat_axis=0, tiled=True)  15.1 us
    dot_general x1, matrix products, body(): jnp.dot(sub_rows, coeffs, preferred_element_type=jnp.float32)  11.7 us
  transfers between devices with their start and end apart: 4, of which 2 were waited for; matrix products, arithmetic and copies ran while one was open for 15% of the time, Pallas kernels for 0%

commit v1 on v0

v1 whole, which is shorter than its diff:
```python
import functools

import jax
import jax.numpy as jnp
from jax import lax
from jax.experimental import pallas as pl
from jax.experimental.pallas import tpu as pltpu
from jax.sharding import PartitionSpec as P

MESH = pl.DeviceIdType.MESH

NX, NZ, NC, NY = 4, 4, 2, 4
NZC = NZ * NC
NB = 16
RR = 16
AHEAD = 4
LAG = 2


def exchange_kernel(
    basis, panels, dest, recv, table, arrived, x_out, relay, pan, pan_f32, product, pick,
    lab_out, lab_relay, lab_in, a_send, a_recv, a_local, x_send, x_recv, z_send, z_recv, z_local,
    p_send, p_recv, l_send, l_recv,
):
    rounds = arrived.shape[0]
    slab, y = lax.axis_index("slab"), lax.axis_index("store")
    x, zc = slab // NZC, slab % NZC
    z, c = zc // NC, zc % NC

    def at_y(d):
        return (slab, (y + d) % NY)

    def x_of(d):
        return (x + d) % NX

    def at_x(d):
        return (x_of(d) * NZC + zc, y)

    def zc_of(d):
        return (z + d // NC) % NZ * NC + (c + d) % NC

    def at_zc(d):
        return (x * NZC + zc_of(d), y)

    def remote(src, dst, send, received, device):
        return pltpu.make_async_remote_copy(
            src_ref=src, dst_ref=dst, send_sem=send, recv_sem=received, device_id=device, device_id_type=MESH
        )

    def wait_bytes(ref, sem):
        pltpu.make_async_copy(ref, ref, sem).wait()

    def start_basis(r):
        rows = pl.ds(pl.multiple_of(r * RR, RR), RR)
        for d in (1, 3, 2):
            remote(
                basis.at[(y + d) % NY, :, rows, :], arrived.at[r, y], a_send, a_recv.at[r], at_y(d)
            ).start()
        pltpu.make_async_copy(basis.at[y, :, rows, :], arrived.at[r, y], a_local.at[r]).start()

    barrier = pltpu.get_barrier_semaphore()
    for d in range(1, NY):
        pl.semaphore_signal(barrier, inc=1, device_id=at_y(d), device_id_type=MESH)
    for d in range(1, NX):
        pl.semaphore_signal(barrier, inc=1, device_id=at_x(d), device_id_type=MESH)
    for d in range(1, NZC):
        pl.semaphore_signal(barrier, inc=1, device_id=at_zc(d), device_id_type=MESH)
    pan_f32[y] = panels[...].astype(jnp.float32)
    pl.semaphore_wait(barrier, NY - 1 + NX - 1 + NZC - 1)

    for d in range(1, NY):
        remote(pan_f32.at[y], pan_f32.at[y], p_send.at[0], p_recv.at[0], at_y(d)).start()
    for r in range(AHEAD):
        start_basis(r)

    def choose(t, _):
        d, q = t // NZC, t % NZC
        target = x_of(d) * NZC + q
        block, place = jnp.int32(0), jnp.int32(-1)
        for b in range(NB):
            value = dest[b]
            hit = value // (NB * NY) == target
            block = jnp.where(hit, b, block)
            place = jnp.where(hit, value % NB, place)
        pick[t] = block
        lab_out[d, q] = jnp.full(lab_out.shape[2:], place, jnp.int32)
        return 0

    lax.fori_loop(0, NX * NZC, choose, 0)
    lab_relay[x] = lab_out[0]
    for d in range(1, NX):
        remote(lab_out.at[d], lab_relay.at[x], l_send.at[0], l_recv.at[0], at_x(d)).start()

    wait_bytes(pan_f32.at[pl.ds(0, NY - 1)], p_recv.at[0])
    pan[x, z, c] = pan_f32[...].reshape(pan.shape[3:]).astype(pan.dtype)
    for d in range(1, NZ):
        remote(pan.at[x, z, c], pan.at[x, z, c], p_send.at[1], p_recv.at[1], at_zc(d * NC)).start()

    wait_bytes(lab_relay.at[pl.ds(0, NX - 1)], l_recv.at[0])
    for d in range(1, NZC):
        remote(lab_relay.at[:, zc_of(d)], lab_in.at[zc], l_send.at[1], l_recv.at[1], at_zc(d)).start()
    lab_in[zc] = lab_relay[:, zc]

    wait_bytes(pan.at[0, pl.ds(0, NZ - 1), 0], p_recv.at[1])
    for d in range(1, NX):
        remote(pan.at[x, :, c], pan.at[x, :, c], p_send.at[2], p_recv.at[2], at_x(d)).start()
    wait_bytes(pan.at[pl.ds(0, NX - 1), :, 0], p_recv.at[2])
    remote(pan.at[:, :, c], pan.at[:, :, c], p_send.at[3], p_recv.at[3], at_zc(1)).start()

    wait_bytes(lab_in.at[pl.ds(0, NZC - 1)], l_recv.at[1])
    lane = lax.broadcasted_iota(jnp.int32, table.shape, 1)
    places = jnp.zeros(table.shape, jnp.int32)
    for q in range(NZC):
        for s in range(NX):
            places = jnp.where(lane == q * NX + s, lab_in[q, s], places)
    table[...] = places

    wait_bytes(pan.at[:, :, 0], p_recv.at[3])

    def one_round(r, _):
        @pl.when(r + AHEAD < rounds)
        def _():
            start_basis(r + AHEAD)

        @pl.when(r < rounds)
        def _():
            wait_bytes(arrived.at[r, pl.ds(0, NY - 1)], a_recv.at[r])
            wait_bytes(arrived.at[r, 0], a_local.at[r])
            total = None
            for s in range(NY):
                left = arrived[r, s].reshape(NB * RR, arrived.shape[-1])
                right = pan[s].reshape(arrived.shape[-1], pan.shape[-1])
                term = jnp.dot(left, right, preferred_element_type=jnp.float32)
                total = term if total is None else total + term
            product[...] = total.astype(product.dtype).reshape(product.shape)
            for d in range(1, NX):
                for q in range(NZC):
                    x_out[r, d - 1, q] = product[pick[d * NZC + q]]
                remote(x_out.at[r, d - 1], relay.at[r, x], x_send, x_recv.at[r], at_x(d)).start()
            for q in range(NZC):
                relay[r, x, q] = product[pick[q]]

        @pl.when(r >= LAG)
        def _():
            k = r - LAG
            rows = pl.ds(pl.multiple_of(k * RR, RR), RR)
            wait_bytes(relay.at[k, pl.ds(0, NX - 1)], x_recv.at[k])
            for d in range(1, NZC):
                remote(relay.at[k, :, zc_of(d)], recv.at[zc, :, rows, :], z_send, z_recv, at_zc(d)).start()
            pltpu.make_async_copy(relay.at[k, :, zc], recv.at[zc, :, rows, :], z_local).start()

        return 0

    lax.fori_loop(0, rounds + LAG, one_round, 0)

    for i in range(3):
        ref = (pan_f32.at[pl.ds(0, NY - 1)], pan.at[0, pl.ds(0, NZ - 1), 0], pan.at[pl.ds(0, NX - 1), :, 0])[i]
        wait_bytes(ref, p_send.at[i])
    wait_bytes(pan.at[:, :, 0], p_send.at[3])
    wait_bytes(lab_relay.at[pl.ds(0, NX - 1)], l_send.at[0])
    wait_bytes(lab_in.at[pl.ds(0, NZC - 1)], l_send.at[1])
    wait_bytes(arrived.at[:, pl.ds(0, NY - 1)], a_send)
    wait_bytes(x_out, x_send)
    wait_bytes(recv.at[0], z_local)
    wait_bytes(recv.at[pl.ds(0, NZC - 1)], z_send)
    wait_bytes(recv.at[pl.ds(0, NZC - 1)], z_recv)


def place_kernel(table, recv, out, held, read_sem, write_sem):
    for s in range(recv.shape[0]):
        place = table[0, s]

        @pl.when(place >= 0)
        def _():
            pltpu.make_async_copy(recv.at[s], held.at[place], read_sem.at[place]).start()

    for p in range(NB):
        pltpu.make_async_copy(recv.at[0], held.at[p], read_sem.at[p]).wait()
        pltpu.make_async_copy(held.at[p], out.at[p], write_sem.at[p]).start()
    for p in range(NB):
        pltpu.make_async_copy(held.at[p], out.at[p], write_sem.at[p]).wait()


def body(basis, panels, dest):
    depth = basis.shape[1]
    cols = panels.shape[1]
    brows = basis.shape[0] // (NY * NB)
    rounds = brows // RR
    bf16 = basis.dtype
    anywhere = pl.BlockSpec(memory_space=pl.ANY)
    vmem = pl.BlockSpec(memory_space=pltpu.VMEM)
    smem = pl.BlockSpec(memory_space=pltpu.SMEM)
    dma = pltpu.SemaphoreType.DMA
    recv, table = pl.pallas_call(
        exchange_kernel,
        out_shape=(
            jax.ShapeDtypeStruct((NZC, NX, brows, cols), bf16),
            jax.ShapeDtypeStruct((8, 128), jnp.int32),
        ),
        in_specs=[anywhere, vmem, smem],
        out_specs=(anywhere, vmem),
        scratch_shapes=[
            pltpu.VMEM((rounds, NY, NB, RR, depth), bf16),
            pltpu.VMEM((rounds, NX - 1, NZC, RR, cols), bf16),
            pltpu.VMEM((rounds, NX, NZC, RR, cols), bf16),
            pltpu.VMEM((NX, NZ, NC, NY * panels.shape[0], cols), bf16),
            pltpu.VMEM((NY, panels.shape[0], cols), jnp.float32),
            pltpu.VMEM((NB, RR, cols), bf16),
            pltpu.SMEM((NX * NZC,), jnp.int32),
            pltpu.VMEM((NX, NZC, 8, 128), jnp.int32),
            pltpu.VMEM((NX, NZC, 8, 128), jnp.int32),
            pltpu.VMEM((NZC, NX, 8, 128), jnp.int32),
            dma, dma((rounds,)), dma((rounds,)), dma, dma((rounds,)), dma, dma, dma,
            dma((4,)), dma((4,)), dma((2,)), dma((2,)),
        ],
        compiler_params=pltpu.CompilerParams(
            collective_id=0, has_side_effects=True, vmem_limit_bytes=56 * 2**20
        ),
    )(basis.reshape(NY, NB, brows, depth), panels, dest)
    out = pl.pallas_call(
        place_kernel,
        out_shape=jax.ShapeDtypeStruct((NB, brows, cols), bf16),
        in_specs=[smem, anywhere],
        out_specs=anywhere,
        scratch_shapes=[pltpu.VMEM((NB, brows, cols), bf16), dma((NB,)), dma((NB,))],
        compiler_params=pltpu.CompilerParams(vmem_limit_bytes=56 * 2**20),
    )(table, recv.reshape(NZC * NX, brows, cols))
    return out.reshape(NB * brows, cols)


def solution(mesh):
    in_specs = (P("slab", "store"), P(("slab", "store"), None), P(("slab", "store")))
    out_specs = P(("slab", "store"), None)
    return jax.shard_map(body, mesh=mesh, in_specs=in_specs, out_specs=out_specs, check_vma=False)
```

time: 508 us -> 179 us (0.35)
  the two profiles are of different devices: /device:TPU:36 before, /device:TPU:1 now
where the time goes in v1:
time: 179 us; the launch traced here: 178 us
  Pallas kernels  178 us (99%)
    pallas_call x1, Pallas kernels, body(): pl.pallas_call(exchange_kernel, out_shape=(jax.ShapeDtypeStruct((NZC, NX,...  172 us
    pallas_call x1, Pallas kernels, body(): pl.pallas_call(place_kernel, out_shape=jax.ShapeDtypeStruct((NB, brows, c...  6.47 us

profile of v1, /device:TPU:1, one launch (start us, length us, event | category | flops | bytes accessed | tf_op | source)
XLA Modules:
  0.0 178.2 jit_solution(8717570744085776201)
XLA Ops:
  0.0 171.7 %shard_map.37 = (bf16[8,4,384,512]{3,2,1,0:T(8,128)(2,1)}, s32[8,128]{1,0:T(8,128)}) custom-call(bf16[4,16,384,256]{3,2,1,0:T(8,128)(2,1)} %bitcast.4, bf16[8,512]{1,0:T(8,128)(2,1)} %panels.1, s32[16]{0:T(128)} %dest.1), custom_call_target="tpu_custom_call" | custom-call | tf_op jit(solution)/shard_map/pallas_call | solution.py:194
  171.7 6.5 %shard_map.38 = bf16[16,384,512]{2,1,0:T(8,128)(2,1)} custom-call(s32[8,128]{1,0:T(8,128)} %get-tuple-element.7.table, bf16[32,384,512]{2,1,0:T(8,128)(2,1)} %bitcast.3), custom_call_target="tpu_custom_call" | custom-call | tf_op jit(solution)/shard_map/pallas_call | solution.py:220

commit v2 on v1

v2 whole, which is shorter than its diff:
```python
import functools

import jax
import jax.numpy as jnp
from jax import lax
from jax.experimental import pallas as pl
from jax.experimental.pallas import tpu as pltpu
from jax.sharding import PartitionSpec as P

MESH = pl.DeviceIdType.MESH

NX, NZ, NC, NY = 4, 4, 2, 4
NZC = NZ * NC
NB = 16
RR = 16
AHEAD = 4
HOPS = (1, 3, 2, 0)
HERE = 6
LAG = 2


def exchange_kernel(
    basis, panels_hbm, dest_hbm, recv, table, panels, dest, arrived, x_out, relay, pan, pan_f32, product, pick,
    lab_out, lab_relay, lab_in, a_send, a_recv, a_local, x_send, x_recv, z_send, z_recv, z_local, in_sem,
    p_send, py_recv, pz_recv, px_recv, pc_recv, l_send, l_recv,
):
    rounds = arrived.shape[0]
    slab, y = lax.axis_index("slab"), lax.axis_index("store")
    x, zc = slab // NZC, slab % NZC
    z, c = zc // NC, zc % NC

    def at_y(d):
        return (slab, (y + d) % NY)

    def x_of(d):
        return (x + d) % NX

    def at_x(d):
        return (x_of(d) * NZC + zc, y)

    def zc_of(q):
        hop = HOPS[q // NC] if isinstance(q, int) else (q // NC == 0) + 3 * (q // NC == 1) + 2 * (q // NC == 2)
        return (z + hop) % NZ * NC + (c + q) % NC

    def at_zc(q):
        return (x * NZC + zc_of(q), y)

    def remote(src, dst, send, received, device):
        return pltpu.make_async_remote_copy(
            src_ref=src, dst_ref=dst, send_sem=send, recv_sem=received, device_id=device, device_id_type=MESH
        )

    def wait_bytes(ref, sem):
        pltpu.make_async_copy(ref, ref, sem).wait()

    def start_basis(r):
        rows = pl.ds(pl.multiple_of(r * RR, RR), RR)
        for d in (1, 3, 2):
            remote(
                basis.at[(y + d) % NY, :, rows, :], arrived.at[r, y], a_send, a_recv.at[r], at_y(d)
            ).start()
        pltpu.make_async_copy(basis.at[y, :, rows, :], arrived.at[r, y], a_local.at[r]).start()

    panels_in = pltpu.make_async_copy(panels_hbm, panels, in_sem.at[0])
    dest_in = pltpu.make_async_copy(dest_hbm, dest, in_sem.at[1])
    panels_in.start()
    dest_in.start()

    barrier = pltpu.get_barrier_semaphore()
    for d in range(1, NY):
        pl.semaphore_signal(barrier, inc=1, device_id=at_y(d), device_id_type=MESH)
    for d in range(1, NX):
        pl.semaphore_signal(barrier, inc=1, device_id=at_x(d), device_id_type=MESH)
    for q in range(NZC):
        if q != HERE:
            pl.semaphore_signal(barrier, inc=1, device_id=at_zc(q), device_id_type=MESH)
    panels_in.wait()
    dest_in.wait()
    pan_f32[y] = panels[...].astype(jnp.float32)
    pl.semaphore_wait(barrier, NY - 1 + NX - 1 + NZC - 1)

    for d in range(1, NY):
        remote(pan_f32.at[y], pan_f32.at[y], p_send.at[0], py_recv, at_y(d)).start()
    for r in range(AHEAD):
        start_basis(r)

    def panels_to_x(chunk):
        for d in (1, 3, 2):
            remote(chunk, chunk, p_send.at[2], px_recv.at[d], at_x(d)).start()

    def panels_to_core(chunk):
        remote(chunk, chunk, p_send.at[3], pc_recv, at_zc(HERE + 1)).start()

    wait_bytes(pan_f32.at[pl.ds(0, NY - 1)], py_recv)
    pan[x, z, c] = pan_f32[...].reshape(pan.shape[3:]).astype(pan.dtype)
    own = pan.at[x, z, c]
    for e in range(NZ - 1):
        remote(own, own, p_send.at[1], pz_recv.at[HOPS[e]], at_zc(e * NC)).start()
    panels_to_x(own)
    panels_to_core(own)
    for d in (1, 3, 2):
        wait_bytes(own, pz_recv.at[d])
        arrived_chunk = pan.at[x, (z + NZ - d) % NZ, c]
        panels_to_x(arrived_chunk)
        panels_to_core(arrived_chunk)

    def choose(t, _):
        d, q = t // NZC, t % NZC
        target = x_of(d) * NZC + zc_of(q)
        block, place = jnp.int32(0), jnp.int32(-1)
        for b in range(NB):
            value = dest[b]
            hit = value // (NB * NY) == target
            block = jnp.where(hit, b, block)
            place = jnp.where(hit, value % NB, place)
        pick[t] = block
        lab_out[d, q] = jnp.full(lab_out.shape[2:], place, jnp.int32)
        return 0

    lax.fori_loop(0, NX * NZC, choose, 0)

    for d in (1, 3, 2):
        wait_bytes(pan.at[0, :, 0], px_recv.at[d])
        panels_to_core(pan.at[x_of(NX - d), :, c])

    lab_relay[x] = lab_out[0]
    for d in range(1, NX):
        remote(lab_out.at[d], lab_relay.at[x], l_send.at[0], l_recv.at[0], at_x(d)).start()

    wait_bytes(pan.at[:, :, 0], pc_recv)

    def one_round(r, _):
        @pl.when(r + AHEAD < rounds)
        def _():
            start_basis(r + AHEAD)

        @pl.when(r < rounds)
        def _():
            wait_bytes(arrived.at[r, pl.ds(0, NY - 1)], a_recv.at[r])
            wait_bytes(arrived.at[r, 0], a_local.at[r])
            total = None
            for s in range(NY):
                left = arrived[r, s].reshape(NB * RR, arrived.shape[-1])
                right = pan[s].reshape(arrived.shape[-1], pan.shape[-1])
                term = jnp.dot(left, right, preferred_element_type=jnp.float32)
                total = term if total is None else total + term
            product[...] = total.astype(product.dtype).reshape(product.shape)
            for d in range(1, NX):
                for q in range(NZC):
                    x_out[r, d - 1, q] = product[pick[d * NZC + q]]
            for h in range(NZ):
                half = pl.ds(h * NC, NC)
                for d in range(1, NX):
                    remote(
                        x_out.at[r, d - 1, half], relay.at[r, x, half], x_send, x_recv.at[r, h], at_x(d)
                    ).start()
            for q in range(NZC):
                relay[r, x, q] = product[pick[q]]

        @pl.when(r >= LAG)
        def _():
            k = r - LAG
            rows = pl.ds(pl.multiple_of(k * RR, RR), RR)
            for h in range(NZ):
                wait_bytes(relay.at[k, pl.ds(0, NX - 1), pl.ds(0, NC)], x_recv.at[k, h])
                for q in range(h * NC, (h + 1) * NC):
                    if q == HERE:
                        pltpu.make_async_copy(relay.at[k, :, q], recv.at[zc, :, rows, :], z_local).start()
                    else:
                        remote(relay.at[k, :, q], recv.at[zc, :, rows, :], z_send, z_recv, at_zc(q)).start()

        @pl.when(r == 1)
        def _():
            wait_bytes(lab_relay.at[pl.ds(0, NX - 1)], l_recv.at[0])
            for q in range(NZC):
                if q != HERE:
                    remote(lab_relay.at[:, q], lab_in.at[zc], l_send.at[1], l_recv.at[1], at_zc(q)).start()
            lab_in[zc] = lab_relay[:, HERE]

        @pl.when(r == 3)
        def _():
            wait_bytes(lab_in.at[pl.ds(0, NZC - 1)], l_recv.at[1])
            lane = lax.broadcasted_iota(jnp.int32, table.shape, 1)
            places = jnp.zeros(table.shape, jnp.int32)
            for q in range(NZC):
                for s in range(NX):
                    places = jnp.where(lane == q * NX + s, lab_in[q, s], places)
            table[...] = places

        return 0

    lax.fori_loop(0, rounds + LAG, one_round, 0)

    wait_bytes(pan_f32.at[pl.ds(0, NY - 1)], p_send.at[0])
    wait_bytes(pan.at[0, pl.ds(0, NZ - 1), 0], p_send.at[1])
    wait_bytes(pan.at[pl.ds(0, NX - 1), :, 0], p_send.at[2])
    wait_bytes(pan.at[:, :, 0], p_send.at[3])
    wait_bytes(lab_relay.at[pl.ds(0, NX - 1)], l_send.at[0])
    wait_bytes(lab_in.at[pl.ds(0, NZC - 1)], l_send.at[1])
    wait_bytes(arrived.at[:, pl.ds(0, NY - 1)], a_send)
    wait_bytes(x_out, x_send)
    wait_bytes(recv.at[0], z_local)
    wait_bytes(recv.at[pl.ds(0, NZC - 1)], z_send)
    wait_bytes(recv.at[pl.ds(0, NZC - 1)], z_recv)


def place_kernel(table, recv, out, sem):
    for s in range(recv.shape[0]):
        place = table[0, s]

        @pl.when(place >= 0)
        def _():
            pltpu.make_async_copy(recv.at[s], out.at[place], sem.at[place]).start()

    for p in range(NB):
        pltpu.make_async_copy(recv.at[0], out.at[p], sem.at[p]).wait()


def body(basis, panels, dest):
    depth = basis.shape[1]
    cols = panels.shape[1]
    brows = basis.shape[0] // (NY * NB)
    rounds = brows // RR
    bf16 = basis.dtype
    anywhere = pl.BlockSpec(memory_space=pl.ANY)
    vmem = pl.BlockSpec(memory_space=pltpu.VMEM)
    smem = pl.BlockSpec(memory_space=pltpu.SMEM)
    in_hbm = pl.BlockSpec(memory_space=pltpu.HBM)
    dma = pltpu.SemaphoreType.DMA
    recv, table = pl.pallas_call(
        exchange_kernel,
        out_shape=(
            jax.ShapeDtypeStruct((NZC, NX, brows, cols), bf16),
            jax.ShapeDtypeStruct((8, 128), jnp.int32),
        ),
        in_specs=[anywhere, in_hbm, in_hbm],
        out_specs=(anywhere, vmem),
        scratch_shapes=[
            pltpu.VMEM(panels.shape, bf16),
            pltpu.SMEM(dest.shape, jnp.int32),
            pltpu.VMEM((rounds, NY, NB, RR, depth), bf16),
            pltpu.VMEM((rounds, NX - 1, NZC, RR, cols), bf16),
            pltpu.VMEM((rounds, NX, NZC, RR, cols), bf16),
            pltpu.VMEM((NX, NZ, NC, NY * panels.shape[0], cols), bf16),
            pltpu.VMEM((NY, panels.shape[0], cols), jnp.float32),
            pltpu.VMEM((NB, RR, cols), bf16),
            pltpu.SMEM((NX * NZC,), jnp.int32),
            pltpu.VMEM((NX, NZC, 8, 128), jnp.int32),
            pltpu.VMEM((NX, NZC, 8, 128), jnp.int32),
            pltpu.VMEM((NZC, NX, 8, 128), jnp.int32),
            dma, dma((rounds,)), dma((rounds,)), dma, dma((rounds, NZ)), dma, dma, dma, dma((2,)),
            dma((4,)), dma, dma((NZ,)), dma((NX,)), dma, dma((2,)), dma((2,)),
        ],
        compiler_params=pltpu.CompilerParams(
            collective_id=0, has_side_effects=True, vmem_limit_bytes=40 * 2**20
        ),
    )(basis.reshape(NY, NB, brows, depth), panels, dest)
    out = pl.pallas_call(
        place_kernel,
        out_shape=jax.ShapeDtypeStruct((NB, brows, cols), bf16),
        in_specs=[smem, anywhere],
        out_specs=anywhere,
        scratch_shapes=[dma((NB,))],
        compiler_params=pltpu.CompilerParams(vmem_limit_bytes=2 * 2**20),
    )(table, recv.reshape(NZC * NX, brows, cols))
    return out.reshape(NB * brows, cols)


def solution(mesh):
    in_specs = (P("slab", "store"), P(("slab", "store"), None), P(("slab", "store")))
    out_specs = P(("slab", "store"), None)
    return jax.shard_map(body, mesh=mesh, in_specs=in_specs, out_specs=out_specs, check_vma=False)
```

time: 179 us -> 171 us (0.955)
  Pallas kernels: 178 us -> 169 us
    pallas_call x1, Pallas kernels: 172 us -> 166 us  [body(): pl.pallas_call(exchange_kernel, out_shape=(jax.ShapeDtypeStruct((NZC, NX,...]
    pallas_call x1, Pallas kernels: 6.47 us -> 3.39 us  [body(): pl.pallas_call(place_kernel, out_shape=jax.ShapeDtypeStruct((NB, brows, c...]
where the time goes in v2:
time: 171 us
  Pallas kernels  169 us (99%)
    pallas_call x1, Pallas kernels, body(): pl.pallas_call(exchange_kernel, out_shape=(jax.ShapeDtypeStruct((NZC, NX,...  166 us

profile of v2, /device:TPU:1, one launch (start us, length us, event | category | flops | bytes accessed | tf_op | source)
XLA Modules:
  0.0 170.8 jit_solution(11394171183568915538)
XLA Ops:
  0.0 0.0 copy-start
  0.0 0.7 copy-done
  0.7 0.0 copy-start.1
  0.7 0.7 copy-done.1
  1.4 166.0 %shard_map.37 = (bf16[8,4,384,512]{3,2,1,0:T(8,128)(2,1)S(1)}, s32[8,128]{1,0:T(8,128)S(1)}) custom-call(bf16[4,16,384,256]{3,2,1,0:T(8,128)(2,1)} %bitcast.4, bf16[8,512]{1,0:T(8,128)(2,1)S(1)} %copy-done, s32[16]{0:T(128)S(1)} %copy-done.1), custom_call_target="tpu_custom_call" | custom-call | tf_op jit(solution)/shard_map/pallas_call | solution.py:230
  167.4 3.4 %shard_map.38 = bf16[16,384,512]{2,1,0:T(8,128)(2,1)} custom-call(s32[8,128]{1,0:T(8,128)S(1)} %get-tuple-element.7.table, bf16[32,384,512]{2,1,0:T(8,128)(2,1)S(1)} %bitcast.3), custom_call_target="tpu_custom_call" | custom-call | tf_op jit(solution)/shard_map/pallas_call | solution.py:258
Async XLA Ops:
  0.0 0.7 copy-start
  0.7 0.7 copy-start.1

commit v3 on v2

--- a/solution.py
+++ b/solution.py
@@ -16,13 +16,13 @@
 AHEAD = 4
 HOPS = (1, 3, 2, 0)
 HERE = 6
-LAG = 2
+NG = 2
 
 
 def exchange_kernel(
     basis, panels_hbm, dest_hbm, recv, table, panels, dest, arrived, x_out, relay, pan, pan_f32, product, pick,
     lab_out, lab_relay, lab_in, a_send, a_recv, a_local, x_send, x_recv, z_send, z_recv, z_local, in_sem,
-    p_send, py_recv, pz_recv, px_recv, pc_recv, l_send, l_recv,
+    p_send, py_recv, p_recv, pc_recv, l_send, l_recv,
 ):
     rounds = arrived.shape[0]
     slab, y = lax.axis_index("slab"), lax.axis_index("store")
@@ -44,6 +44,9 @@
 
     def at_zc(q):
         return (x * NZC + zc_of(q), y)
+
+    def at_xz(d, e):
+        return (x_of(d) * NZC + zc_of(e * NC), y)
 
     def remote(src, dst, send, received, device):
         return pltpu.make_async_remote_copy(
@@ -71,38 +74,41 @@
         pl.semaphore_signal(barrier, inc=1, device_id=at_y(d), device_id_type=MESH)
     for d in range(1, NX):
         pl.semaphore_signal(barrier, inc=1, device_id=at_x(d), device_id_type=MESH)
+    for d in range(1, NX):
+        for e in range(NZ - 1):
+            pl.semaphore_signal(barrier, inc=1, device_id=at_xz(d, e), device_id_type=MESH)
     for q in range(NZC):
         if q != HERE:
             pl.semaphore_signal(barrier, inc=1, device_id=at_zc(q), device_id_type=MESH)
     panels_in.wait()
     dest_in.wait()
     pan_f32[y] = panels[...].astype(jnp.float32)
-    pl.semaphore_wait(barrier, NY - 1 + NX - 1 + NZC - 1)
+    pl.semaphore_wait(barrier, NY - 1 + NX - 1 + (NX - 1) * (NZ - 1) + NZC - 1)
 
     for d in range(1, NY):
-        remote(pan_f32.at[y], pan_f32.at[y], p_send.at[0], py_recv, at_y(d)).start()
+        remote(pan_f32.at[y], pan_f32.at[y], p_send.at[0, 0], py_recv, at_y(d)).start()
     for r in range(AHEAD):
         start_basis(r)
 
-    def panels_to_x(chunk):
-        for d in (1, 3, 2):
-            remote(chunk, chunk, p_send.at[2], px_recv.at[d], at_x(d)).start()
-
-    def panels_to_core(chunk):
-        remote(chunk, chunk, p_send.at[3], pc_recv, at_zc(HERE + 1)).start()
-
+    width = pan.shape[-1]
     wait_bytes(pan_f32.at[pl.ds(0, NY - 1)], py_recv)
-    pan[x, z, c] = pan_f32[...].reshape(pan.shape[3:]).astype(pan.dtype)
-    own = pan.at[x, z, c]
-    for e in range(NZ - 1):
-        remote(own, own, p_send.at[1], pz_recv.at[HOPS[e]], at_zc(e * NC)).start()
-    panels_to_x(own)
-    panels_to_core(own)
-    for d in (1, 3, 2):
-        wait_bytes(own, pz_recv.at[d])
-        arrived_chunk = pan.at[x, (z + NZ - d) % NZ, c]
-        panels_to_x(arrived_chunk)
-        panels_to_core(arrived_chunk)
+    for g in range(NG):
+        part = pan_f32[:, :, g * width : (g + 1) * width]
+        pan[g, x, z, c] = part.reshape(pan.shape[4:]).astype(pan.dtype)
+        own = pan.at[g, x, z, c]
+        for d in (2, 1, 3):
+            for e in (2, 0, 1):
+                remote(own, own, p_send.at[1, g], p_recv.at[0, g], at_xz(d, e)).start()
+            remote(own, own, p_send.at[2, g], p_recv.at[1, g], at_x(d)).start()
+        for e in (2, 0, 1):
+            remote(own, own, p_send.at[3, g], p_recv.at[2, g], at_zc(e * NC)).start()
+
+    def panels_in_line(g):
+        wait_bytes(pan.at[g, pl.ds(0, NX - 1), pl.ds(0, NZ - 1), 0], p_recv.at[0, g])
+        wait_bytes(pan.at[g, pl.ds(0, NX - 1), 0, 0], p_recv.at[1, g])
+        wait_bytes(pan.at[g, 0, pl.ds(0, NZ - 1), 0], p_recv.at[2, g])
+        half = pan.at[g, :, :, c]
+        remote(half, half, p_send.at[4, g], pc_recv.at[g], at_zc(HERE + 1)).start()
 
     def choose(t, _):
         d, q = t // NZC, t % NZC
@@ -119,15 +125,23 @@
 
     lax.fori_loop(0, NX * NZC, choose, 0)
 
-    for d in (1, 3, 2):
-        wait_bytes(pan.at[0, :, 0], px_recv.at[d])
-        panels_to_core(pan.at[x_of(NX - d), :, c])
-
+    panels_in_line(0)
     lab_relay[x] = lab_out[0]
     for d in range(1, NX):
         remote(lab_out.at[d], lab_relay.at[x], l_send.at[0], l_recv.at[0], at_x(d)).start()
 
-    wait_bytes(pan.at[:, :, 0], pc_recv)
+    panels_in_line(1)
+    wait_bytes(pan.at[0, :, :, 0], pc_recv.at[0])
+
+    def forward(r, g, h):
+        rows, columns = pl.ds(pl.multiple_of(r * RR, RR), RR), pl.ds(g * width, width)
+        wait_bytes(relay.at[r, g, pl.ds(0, NX - 1), pl.ds(0, NZC // 2)], x_recv.at[r, g, h])
+        for q in range(h * (NZC // 2), (h + 1) * (NZC // 2)):
+            src, dst = relay.at[r, g, :, q], recv.at[zc, :, rows, columns]
+            if q == HERE:
+                pltpu.make_async_copy(src, dst, z_local).start()
+            else:
+                remote(src, dst, z_send, z_recv, at_zc(q)).start()
 
     def one_round(r, _):
         @pl.when(r + AHEAD < rounds)
@@ -138,36 +152,40 @@
         def _():
             wait_bytes(arrived.at[r, pl.ds(0, NY - 1)], a_recv.at[r])
             wait_bytes(arrived.at[r, 0], a_local.at[r])
-            total = None
-            for s in range(NY):
-                left = arrived[r, s].reshape(NB * RR, arrived.shape[-1])
-                right = pan[s].reshape(arrived.shape[-1], pan.shape[-1])
-                term = jnp.dot(left, right, preferred_element_type=jnp.float32)
-                total = term if total is None else total + term
-            product[...] = total.astype(product.dtype).reshape(product.shape)
-            for d in range(1, NX):
+            for g in range(NG):
+                if g == 1:
+
+                    @pl.when(r == 0)
+                    def _():
+                        wait_bytes(pan.at[1, :, :, 0], pc_recv.at[1])
+
+                total = None
+                for s in range(NY):
+                    left = arrived[r, s].reshape(NB * RR, arrived.shape[-1])
+                    right = pan[g, s].reshape(arrived.shape[-1], width)
+                    term = jnp.dot(left, right, preferred_element_type=jnp.float32)
+                    total = term if total is None else total + term
+                product[...] = total.astype(product.dtype).reshape(product.shape)
+                for d in range(1, NX):
+                    for q in range(NZC):
+                        x_out[r, g, d - 1, q] = product[pick[d * NZC + q]]
+                for h in range(2):
+                    half = pl.ds(h * (NZC // 2), NZC // 2)
+                    for d in (1, 3, 2):
+                        remote(
+                            x_out.at[r, g, d - 1, half], relay.at[r, g, x, half], x_send, x_recv.at[r, g, h], at_x(d)
+                        ).start()
                 for q in range(NZC):
-                    x_out[r, d - 1, q] = product[pick[d * NZC + q]]
-            for h in range(NZ):
-                half = pl.ds(h * NC, NC)
-                for d in range(1, NX):
-                    remote(
-                        x_out.at[r, d - 1, half], relay.at[r, x, half], x_send, x_recv.at[r, h], at_x(d)
-                    ).start()
-            for q in range(NZC):
-                relay[r, x, q] = product[pick[q]]
-
-        @pl.when(r >= LAG)
-        def _():
-            k = r - LAG
-            rows = pl.ds(pl.multiple_of(k * RR, RR), RR)
-            for h in range(NZ):
-                wait_bytes(relay.at[k, pl.ds(0, NX - 1), pl.ds(0, NC)], x_recv.at[k, h])
-                for q in range(h * NC, (h + 1) * NC):
-                    if q == HERE:
-                        pltpu.make_async_copy(relay.at[k, :, q], recv.at[zc, :, rows, :], z_local).start()
-                    else:
-                        remote(relay.at[k, :, q], recv.at[zc, :, rows, :], z_send, z_recv, at_zc(q)).start()
+                    relay[r, g, x, q] = product[pick[q]]
+
+        @pl.when(r >= 1)
+        def _():
+            for g, h in ((0, 1), (1, 0), (1, 1)):
+                forward(r - 1, g, h)
+
+        @pl.when(r < rounds)
+        def _():
+            forward(r, 0, 0)
 
         @pl.when(r == 1)
         def _():
@@ -189,12 +207,14 @@
 
         return 0
 
-    lax.fori_loop(0, rounds + LAG, one_round, 0)
-
-    wait_bytes(pan_f32.at[pl.ds(0, NY - 1)], p_send.at[0])
-    wait_bytes(pan.at[0, pl.ds(0, NZ - 1), 0], p_send.at[1])
-    wait_bytes(pan.at[pl.ds(0, NX - 1), :, 0], p_send.at[2])
-    wait_bytes(pan.at[:, :, 0], p_send.at[3])
+    lax.fori_loop(0, rounds + 1, one_round, 0)
+
+    wait_bytes(pan_f32.at[pl.ds(0, NY - 1)], p_send.at[0, 0])
+    for g in range(NG):
+        wait_bytes(pan.at[g, pl.ds(0, NX - 1), pl.ds(0, NZ - 1), 0], p_send.at[1, g])
+        wait_bytes(pan.at[g, pl.ds(0, NX - 1), 0, 0], p_send.at[2, g])
+        wait_bytes(pan.at[g, 0, pl.ds(0, NZ - 1), 0], p_send.at[3, g])
+        wait_bytes(pan.at[g, :, :, 0], p_send.at[4, g])
     wait_bytes(lab_relay.at[pl.ds(0, NX - 1)], l_send.at[0])
     wait_bytes(lab_in.at[pl.ds(0, NZC - 1)], l_send.at[1])
     wait_bytes(arrived.at[:, pl.ds(0, NY - 1)], a_send)
@@ -226,6 +246,7 @@
     vmem = pl.BlockSpec(memory_space=pltpu.VMEM)
     smem = pl.BlockSpec(memory_space=pltpu.SMEM)
     in_hbm = pl.BlockSpec(memory_space=pltpu.HBM)
+    hbm = lambda a: pltpu.with_memory_space_constraint(a, pltpu.HBM)
     dma = pltpu.SemaphoreType.DMA
     recv, table = pl.pallas_call(
         exchange_kernel,
@@ -239,22 +260,22 @@
             pltpu.VMEM(panels.shape, bf16),
             pltpu.SMEM(dest.shape, jnp.int32),
             pltpu.VMEM((rounds, NY, NB, RR, depth), bf16),
-            pltpu.VMEM((rounds, NX - 1, NZC, RR, cols), bf16),
-            pltpu.VMEM((rounds, NX, NZC, RR, cols), bf16),
-            pltpu.VMEM((NX, NZ, NC, NY * panels.shape[0], cols), bf16),
+            pltpu.VMEM((rounds, NG, NX - 1, NZC, RR, cols // NG), bf16),
+            pltpu.VMEM((rounds, NG, NX, NZC, RR, cols // NG), bf16),
+            pltpu.VMEM((NG, NX, NZ, NC, NY * panels.shape[0], cols // NG), bf16),
             pltpu.VMEM((NY, panels.shape[0], cols), jnp.float32),
-            pltpu.VMEM((NB, RR, cols), bf16),
+            pltpu.VMEM((NB, RR, cols // NG), bf16),
             pltpu.SMEM((NX * NZC,), jnp.int32),
             pltpu.VMEM((NX, NZC, 8, 128), jnp.int32),
             pltpu.VMEM((NX, NZC, 8, 128), jnp.int32),
             pltpu.VMEM((NZC, NX, 8, 128), jnp.int32),
-            dma, dma((rounds,)), dma((rounds,)), dma, dma((rounds, NZ)), dma, dma, dma, dma((2,)),
-            dma((4,)), dma, dma((NZ,)), dma((NX,)), dma, dma((2,)), dma((2,)),
+            dma, dma((rounds,)), dma((rounds,)), dma, dma((rounds, NG, 2)), dma, dma, dma, dma((2,)),
+            dma((5, NG)), dma, dma((3, NG)), dma((NG,)), dma((2,)), dma((2,)),
         ],
         compiler_params=pltpu.CompilerParams(
             collective_id=0, has_side_effects=True, vmem_limit_bytes=40 * 2**20
         ),
-    )(basis.reshape(NY, NB, brows, depth), panels, dest)
+    )(basis.reshape(NY, NB, brows, depth), hbm(panels), hbm(dest))
     out = pl.pallas_call(
         place_kernel,
         out_shape=jax.ShapeDtypeStruct((NB, brows, cols), bf16),

time: 171 us -> 169 us (0.988)
  no operation moved by 1% of the time
where the time goes in v3:
time: 169 us
  Pallas kernels  168 us (99%)
    pallas_call x1, Pallas kernels, body(): pl.pallas_call(exchange_kernel, out_shape=(jax.ShapeDtypeStruct((NZC, NX,...  165 us
    pallas_call x1, Pallas kernels, body(): pl.pallas_call(place_kernel, out_shape=jax.ShapeDtypeStruct((NB, brows, c...  3.4 us

profile of v3, /device:TPU:1, one launch (start us, length us, event | category | flops | bytes accessed | tf_op | source)
XLA Modules:
  0.0 168.5 jit_solution(9469443945876694971)
XLA Ops:
  0.0 165.1 %shard_map.37 = (bf16[8,4,384,512]{3,2,1,0:T(8,128)(2,1)S(1)}, s32[8,128]{1,0:T(8,128)S(1)}) custom-call(bf16[4,16,384,256]{3,2,1,0:T(8,128)(2,1)} %bitcast.4, bf16[8,512]{1,0:T(8,128)(2,1)} %panels_hbm.1, s32[16]{0:T(128)} %dest_hbm.1), custom_call_target="tpu_custom_call" | custom-call | tf_op jit(solution)/shard_map/pallas_call | solution.py:251
  165.1 3.4 %shard_map.38 = bf16[16,384,512]{2,1,0:T(8,128)(2,1)} custom-call(s32[8,128]{1,0:T(8,128)S(1)} %get-tuple-element.7.table, bf16[32,384,512]{2,1,0:T(8,128)(2,1)S(1)} %bitcast.3), custom_call_target="tpu_custom_call" | custom-call | tf_op jit(solution)/shard_map/pallas_call | solution.py:279

commit v4 on v3

--- a/solution.py
+++ b/solution.py
@@ -16,12 +16,13 @@
 AHEAD = 4
 HOPS = (1, 3, 2, 0)
 HERE = 6
-NG = 2
+SENT = (0, 1, 2, 3, 4, 5, 7)
+NG = 4
 
 
 def exchange_kernel(
-    basis, panels_hbm, dest_hbm, recv, table, panels, dest, arrived, x_out, relay, pan, pan_f32, product, pick,
-    lab_out, lab_relay, lab_in, a_send, a_recv, a_local, x_send, x_recv, z_send, z_recv, z_local, in_sem,
+    basis, panels_hbm, dest_hbm, recv, table, panels, dest, arrived, x_out, x_relay, z_out, z_relay, pan, pan_f32, product, pick,
+    lab_out, lab_relay, lab_in, a_send, a_recv, a_local, x_send, x_recv, z_send, z_recv, z2_send, z2_recv, x2_send, x2_recv, local, in_sem,
     p_send, py_recv, p_recv, pc_recv, l_send, l_recv,
 ):
     rounds = arrived.shape[0]
@@ -130,18 +131,21 @@
     for d in range(1, NX):
         remote(lab_out.at[d], lab_relay.at[x], l_send.at[0], l_recv.at[0], at_x(d)).start()
 
-    panels_in_line(1)
-    wait_bytes(pan.at[0, :, :, 0], pc_recv.at[0])
-
-    def forward(r, g, h):
+    def forward(r, g):
         rows, columns = pl.ds(pl.multiple_of(r * RR, RR), RR), pl.ds(g * width, width)
-        wait_bytes(relay.at[r, g, pl.ds(0, NX - 1), pl.ds(0, NZC // 2)], x_recv.at[r, g, h])
-        for q in range(h * (NZC // 2), (h + 1) * (NZC // 2)):
-            src, dst = relay.at[r, g, :, q], recv.at[zc, :, rows, columns]
-            if q == HERE:
-                pltpu.make_async_copy(src, dst, z_local).start()
-            else:
-                remote(src, dst, z_send, z_recv, at_zc(q)).start()
+        k = g // 2
+        if g % 2 == 0:
+            wait_bytes(x_relay.at[r, k, pl.ds(0, NX - 1)], x_recv.at[r, k])
+            dst = recv.at[zc, :, rows, columns]
+            for q in SENT:
+                remote(x_relay.at[r, k, :, q], dst, z2_send, z2_recv, at_zc(q)).start()
+            pltpu.make_async_copy(x_relay.at[r, k, :, HERE], dst, local.at[0]).start()
+        else:
+            wait_bytes(z_relay.at[r, k, pl.ds(0, NZC - 1)], z_recv.at[r, k])
+            dst = recv.at[:, x, rows, columns]
+            for d in (1, 3, 2):
+                remote(z_relay.at[r, k, :, d], dst, x2_send, x2_recv, at_x(d)).start()
+            pltpu.make_async_copy(z_relay.at[r, k, :, 0], dst, local.at[1]).start()
 
     def one_round(r, _):
         @pl.when(r + AHEAD < rounds)
@@ -153,11 +157,11 @@
             wait_bytes(arrived.at[r, pl.ds(0, NY - 1)], a_recv.at[r])
             wait_bytes(arrived.at[r, 0], a_local.at[r])
             for g in range(NG):
-                if g == 1:
-
-                    @pl.when(r == 0)
-                    def _():
-                        wait_bytes(pan.at[1, :, :, 0], pc_recv.at[1])
+                @pl.when(r == 0)
+                def _():
+                    if g + 1 < NG:
+                        panels_in_line(g + 1)
+                    wait_bytes(pan.at[g, :, :, 0], pc_recv.at[g])
 
                 total = None
                 for s in range(NY):
@@ -166,26 +170,33 @@
                     term = jnp.dot(left, right, preferred_element_type=jnp.float32)
                     total = term if total is None else total + term
                 product[...] = total.astype(product.dtype).reshape(product.shape)
-                for d in range(1, NX):
-                    for q in range(NZC):
-                        x_out[r, g, d - 1, q] = product[pick[d * NZC + q]]
-                for h in range(2):
-                    half = pl.ds(h * (NZC // 2), NZC // 2)
+                k = g // 2
+                if g % 2 == 0:
+                    for d in range(1, NX):
+                        for q in range(NZC):
+                            x_out[r, k, d - 1, q] = product[pick[d * NZC + q]]
                     for d in (1, 3, 2):
                         remote(
-                            x_out.at[r, g, d - 1, half], relay.at[r, g, x, half], x_send, x_recv.at[r, g, h], at_x(d)
+                            x_out.at[r, k, d - 1], x_relay.at[r, k, x], x_send, x_recv.at[r, k], at_x(d)
                         ).start()
-                for q in range(NZC):
-                    relay[r, g, x, q] = product[pick[q]]
+                    for q in range(NZC):
+                        x_relay[r, k, x, q] = product[pick[q]]
+                else:
+                    for q in range(NZC):
+                        for d in range(NX):
+                            if q == HERE:
+                                z_relay[r, k, zc, d] = product[pick[d * NZC + q]]
+                            else:
+                                z_out[r, k, SENT.index(q), d] = product[pick[d * NZC + q]]
+                    for i, q in enumerate(SENT):
+                        remote(
+                            z_out.at[r, k, i], z_relay.at[r, k, zc], z_send, z_recv.at[r, k], at_zc(q)
+                        ).start()
 
         @pl.when(r >= 1)
         def _():
-            for g, h in ((0, 1), (1, 0), (1, 1)):
-                forward(r - 1, g, h)
-
-        @pl.when(r < rounds)
-        def _():
-            forward(r, 0, 0)
+            for g in range(NG):
+                forward(r - 1, g)
 
         @pl.when(r == 1)
         def _():
@@ -219,9 +230,14 @@
     wait_bytes(lab_in.at[pl.ds(0, NZC - 1)], l_send.at[1])
     wait_bytes(arrived.at[:, pl.ds(0, NY - 1)], a_send)
     wait_bytes(x_out, x_send)
-    wait_bytes(recv.at[0], z_local)
-    wait_bytes(recv.at[pl.ds(0, NZC - 1)], z_send)
-    wait_bytes(recv.at[pl.ds(0, NZC - 1)], z_recv)
+    half = pl.ds(0, NG // 2 * width)
+    wait_bytes(z_out, z_send)
+    wait_bytes(recv.at[0, :, :, half], local.at[0])
+    wait_bytes(recv.at[:, 0, :, half], local.at[1])
+    wait_bytes(recv.at[pl.ds(0, NZC - 1), :, :, half], z2_send)
+    wait_bytes(recv.at[:, pl.ds(0, NX - 1), :, half], x2_send)
+    wait_bytes(recv.at[pl.ds(0, NZC - 1), :, :, half], z2_recv)
+    wait_bytes(recv.at[:, pl.ds(0, NX - 1), :, half], x2_recv)
 
 
 def place_kernel(table, recv, out, sem):
@@ -260,8 +276,10 @@
             pltpu.VMEM(panels.shape, bf16),
             pltpu.SMEM(dest.shape, jnp.int32),
             pltpu.VMEM((rounds, NY, NB, RR, depth), bf16),
-            pltpu.VMEM((rounds, NG, NX - 1, NZC, RR, cols // NG), bf16),
-            pltpu.VMEM((rounds, NG, NX, NZC, RR, cols // NG), bf16),
+            pltpu.VMEM((rounds, NG // 2, NX - 1, NZC, RR, cols // NG), bf16),
+            pltpu.VMEM((rounds, NG // 2, NX, NZC, RR, cols // NG), bf16),
+            pltpu.VMEM((rounds, NG // 2, NZC - 1, NX, RR, cols // NG), bf16),
+            pltpu.VMEM((rounds, NG // 2, NZC, NX, RR, cols // NG), bf16),
             pltpu.VMEM((NG, NX, NZ, NC, NY * panels.shape[0], cols // NG), bf16),
             pltpu.VMEM((NY, panels.shape[0], cols), jnp.float32),
             pltpu.VMEM((NB, RR, cols // NG), bf16),
@@ -269,7 +287,8 @@
             pltpu.VMEM((NX, NZC, 8, 128), jnp.int32),
             pltpu.VMEM((NX, NZC, 8, 128), jnp.int32),
             pltpu.VMEM((NZC, NX, 8, 128), jnp.int32),
-            dma, dma((rounds,)), dma((rounds,)), dma, dma((rounds, NG, 2)), dma, dma, dma, dma((2,)),
+            dma, dma((rounds,)), dma((rounds,)), dma, dma((rounds, NG // 2)), dma, dma((rounds, NG // 2)),
+            dma, dma, dma, dma, dma((2,)), dma((2,)),
             dma((5, NG)), dma, dma((3, NG)), dma((NG,)), dma((2,)), dma((2,)),
         ],
         compiler_params=pltpu.CompilerParams(

time: 169 us -> 165 us (0.976)
  Pallas kernels: 168 us -> 165 us
    pallas_call x1, Pallas kernels: 165 us -> 161 us  [body(): pl.pallas_call(exchange_kernel, out_shape=(jax.ShapeDtypeStruct((NZC, NX,...]
where the time goes in v4:
time: 165 us
  Pallas kernels  165 us (100%)
    pallas_call x1, Pallas kernels, body(): pl.pallas_call(exchange_kernel, out_shape=(jax.ShapeDtypeStruct((NZC, NX,...  161 us
    pallas_call x1, Pallas kernels, body(): pl.pallas_call(place_kernel, out_shape=jax.ShapeDtypeStruct((NB, brows, c...  3.41 us

profile of v4, /device:TPU:1, one launch (start us, length us, event | category | flops | bytes accessed | tf_op | source)
XLA Modules:
  0.0 164.6 jit_solution(15170073917340966302)
XLA Ops:
  0.0 161.2 %shard_map.37 = (bf16[8,4,384,512]{3,2,1,0:T(8,128)(2,1)S(1)}, s32[8,128]{1,0:T(8,128)S(1)}) custom-call(bf16[4,16,384,256]{3,2,1,0:T(8,128)(2,1)} %bitcast.4, bf16[8,512]{1,0:T(8,128)(2,1)} %panels_hbm.1, s32[16]{0:T(128)} %dest_hbm.1), custom_call_target="tpu_custom_call" | custom-call | tf_op jit(solution)/shard_map/pallas_call | solution.py:267
  161.2 3.4 %shard_map.38 = bf16[16,384,512]{2,1,0:T(8,128)(2,1)} custom-call(s32[8,128]{1,0:T(8,128)S(1)} %get-tuple-element.7.table, bf16[32,384,512]{2,1,0:T(8,128)(2,1)S(1)} %bitcast.3), custom_call_target="tpu_custom_call" | custom-call | tf_op jit(solution)/shard_map/pallas_call | solution.py:298

commit v5 on v4

--- a/solution.py
+++ b/solution.py
@@ -268,7 +268,7 @@
         exchange_kernel,
         out_shape=(
             jax.ShapeDtypeStruct((NZC, NX, brows, cols), bf16),
-            jax.ShapeDtypeStruct((8, 128), jnp.int32),
+            jax.ShapeDtypeStruct((1, 128), jnp.int32),
         ),
         in_specs=[anywhere, in_hbm, in_hbm],
         out_specs=(anywhere, vmem),
@@ -284,9 +284,9 @@
             pltpu.VMEM((NY, panels.shape[0], cols), jnp.float32),
             pltpu.VMEM((NB, RR, cols // NG), bf16),
             pltpu.SMEM((NX * NZC,), jnp.int32),
-            pltpu.VMEM((NX, NZC, 8, 128), jnp.int32),
-            pltpu.VMEM((NX, NZC, 8, 128), jnp.int32),
-            pltpu.VMEM((NZC, NX, 8, 128), jnp.int32),
+            pltpu.VMEM((NX, NZC, 1, 128), jnp.int32),
+            pltpu.VMEM((NX, NZC, 1, 128), jnp.int32),
+            pltpu.VMEM((NZC, NX, 1, 128), jnp.int32),
             dma, dma((rounds,)), dma((rounds,)), dma, dma((rounds, NG // 2)), dma, dma((rounds, NG // 2)),
             dma, dma, dma, dma, dma((2,)), dma((2,)),
             dma((5, NG)), dma, dma((3, NG)), dma((NG,)), dma((2,)), dma((2,)),

time: 165 us -> 163 us (0.988)
  Pallas kernels: 165 us -> 163 us
where the time goes in v5:
time: 163 us
  Pallas kernels  163 us (100%)
    pallas_call x1, Pallas kernels, body(): pl.pallas_call(exchange_kernel, out_shape=(jax.ShapeDtypeStruct((NZC, NX,...  160 us
    pallas_call x1, Pallas kernels, body(): pl.pallas_call(place_kernel, out_shape=jax.ShapeDtypeStruct((NB, brows, c...  3.33 us

profile of v5, /device:TPU:1, one launch (start us, length us, event | category | flops | bytes accessed | tf_op | source)
XLA Modules:
  0.0 163.1 jit_solution(16377738720066319552)
XLA Ops:
  0.0 159.8 %shard_map.37 = (bf16[8,4,384,512]{3,2,1,0:T(8,128)(2,1)S(1)}, s32[1,128]{1,0:T(1,128)S(1)}) custom-call(bf16[4,16,384,256]{3,2,1,0:T(8,128)(2,1)} %bitcast.4, bf16[8,512]{1,0:T(8,128)(2,1)} %panels_hbm.1, s32[16]{0:T(128)} %dest_hbm.1), custom_call_target="tpu_custom_call" | custom-call | tf_op jit(solution)/shard_map/pallas_call | solution.py:267
  159.8 3.3 %shard_map.38 = bf16[16,384,512]{2,1,0:T(8,128)(2,1)} custom-call(s32[1,128]{1,0:T(1,128)S(1)} %get-tuple-element.7.table, bf16[32,384,512]{2,1,0:T(8,128)(2,1)S(1)} %bitcast.3), custom_call_target="tpu_custom_call" | custom-call | tf_op jit(solution)/shard_map/pallas_call | solution.py:298
